TPU v7x, 256 devices: a whole 4x4x8 slice. The times are simulated.
256 devices in a mesh: rows: 64 (over x, z, core), cols: 4 (over y).
Axes of the slice: x: 4, y: 4, z: 8, core: 2. Of those that a mesh axis runs over, the one named last changes fastest.
Arguments:
- embeddings: float32 [131072, 128], P('rows'), may hold values from -8 to 8
- centres: float32 [8192, 128], P('cols'), may hold values from -24 to 24
Outputs:
- new_centres: float32 [8192, 128], P('cols')
- expected_similarity: float32 [131072], P('rows')
All inputs are finite; a program needn't handle non-finite values.
Results may differ from a plain program's by a relative error of at most 0.0003.
Values sent between devices are 32-bit elements; how exact they have to be, the bound alone decides.
A program may use at most 128 MiB of HBM per device.

v0:
```python
import jax
import jax.numpy as jnp
from jax import lax
from jax.sharding import PartitionSpec as P

ITERS = 3


inverse_temp = 20.0


def unit_rows(value):
    return value * lax.rsqrt(jnp.sum(value * value, axis=-1, keepdims=True) + 1e-06)


def local(embeddings, centres):
    unit_x = unit_rows(embeddings)
    unit_c = unit_rows(centres)
    rows_here = unit_x.shape[0]
    clu_here = unit_c.shape[0]
    mol_count = rows_here * lax.axis_size("rows")
    clu_count = clu_here * lax.axis_size("cols")
    scores = jnp.dot(
        unit_x, unit_c.T, precision=lax.Precision.HIGHEST, preferred_element_type=jnp.float32
    )
    expo = jnp.exp(scores * inverse_temp)
    row_scale = jnp.ones((rows_here,), jnp.float32)
    for step in range(ITERS):
        partial_value = jnp.dot(row_scale, expo, precision=lax.Precision.HIGHEST)
        col_mass = lax.psum(partial_value, "rows")
        col_scale = 1.0 / clu_count / col_mass
        row_part = jnp.dot(expo, col_scale, precision=lax.Precision.HIGHEST)
        if step + 1 < ITERS:
            row_sum = lax.psum(row_part, "cols")
        else:
            numer_part = jnp.dot(expo * scores, col_scale, precision=lax.Precision.HIGHEST)
            row_sum, numer = lax.psum((row_part, numer_part), "cols")
        row_scale = 1.0 / mol_count / row_sum
    expected = numer / row_sum
    inv_rows = 1.0 / row_sum
    weights = expo * col_scale[None, :] * inv_rows[:, None]
    sums = jnp.dot(
        weights.T, unit_x, precision=lax.Precision.HIGHEST, preferred_element_type=jnp.float32
    )
    total = lax.psum(sums, "rows")
    new_centres = unit_rows(total)
    return (new_centres, expected)


def solution(mesh):
    placed = (P("rows", None), P("cols", None))
    return jax.shard_map(
        local, mesh=mesh, in_specs=placed, out_specs=(P("cols", None), P("rows")), check_vma=False
    )
```

profile of v0, /device:TPU:1, one launch (start us, length us, event | category | flops | bytes accessed | tf_op | source)
XLA Modules:
  0.0 786.8 jit_solution(11491713770881462800)
XLA Ops:
  7.2 0.0 all-reduce.3.cloned.1.call-start
  7.2 1.6 multiply_reduce_fusion.1
  8.8 1.6 multiply_reduce_fusion.2
  10.4 16.0 %fusion.21 = f32[2048,2048]{1,0:T(8,128)S(1)} fusion(f32[2048,128]{1,0:T(8,128)} %param.3, f32[2048,128]{1,0:T(8,128)} %param.2, f32[2048]{0:T(1024)S(1)} %get-tuple-element.6, f32[2048]{0:T(1024)S(1)} %get-tuple-element.7), kind=kOutput, calls=%fused_computation.23 | convolution fusion | flops 6442975232 | bytes 18890752 | tf_op jit(solution)/shard_map/dot_general | solution.py:23
  26.4 5.7 copy-done
  32.1 9.6 %fusion.10 = f32[1,2048]{1,0:T(1,128)S(1)} fusion(f32[2048,2048]{1,0:T(8,128)S(1)} %fusion.21), kind=kOutput, calls=%fused_computation.11 | convolution fusion | flops 54525952 | bytes 16785408 | tf_op jit(solution)/shard_map/dot_general | solution.py:29
  41.7 130.0 %psum.56 = f32[2048]{0:T(1024)S(1)} all-reduce(f32[2048]{0:T(1024)S(1)} %bitcast.31), channel_id=1, replica_groups=mesh['rows'=64,'cols'=4] {'rows'}, use_global_device_ids=true, to_apply=%region_2.0 | all-reduce | flops 2048 | bytes 16384 | tf_op jit(solution)/shard_map/psum | solution.py:30
  171.7 19.1 %fusion.9 = f32[1,2048]{1,0:T(1,128)S(1)} fusion(f32[2048,1]{0,1:T(1,128)S(1)} %bitcast.25, f32[2048,2048]{1,0:T(8,128)} %copy-done), kind=kOutput, calls=%fused_computation.10 | convolution fusion | flops 54525952 | bytes 16793600 | tf_op jit(solution)/shard_map/dot_general | solution.py:32
  190.8 8.8 %psum.57 = f32[2048]{0:T(1024)S(1)} all-reduce(f32[2048]{0:T(1024)S(1)} %bitcast.23), channel_id=1, replica_groups=mesh['rows'=64,'cols'=4] {'cols'}, use_global_device_ids=true, to_apply=%region_3.0 | all-reduce | flops 2048 | bytes 16384 | tf_op jit(solution)/shard_map/psum | solution.py:34
  199.6 12.9 %fusion.8 = f32[1,2048]{1,0:T(1,128)S(1)} fusion(f32[2048,1]{0,1:T(1,128)S(1)} %bitcast.26, f32[2048,2048]{1,0:T(8,128)} %copy-done), kind=kOutput, calls=%fused_computation.9 | convolution fusion | flops 54525952 | bytes 16793600 | tf_op jit(solution)/shard_map/dot_general | solution.py:29
  212.5 132.9 %psum.58 = f32[2048]{0:T(1024)S(1)} all-reduce(f32[2048]{0:T(1024)S(1)} %bitcast.27), channel_id=1, replica_groups=mesh['rows'=64,'cols'=4] {'rows'}, use_global_device_ids=true, to_apply=%region_4.0 | all-reduce | flops 2048 | bytes 16384 | tf_op jit(solution)/shard_map/psum | solution.py:30
  345.4 19.1 %fusion.7 = f32[1,2048]{1,0:T(1,128)S(1)} fusion(f32[2048,1]{0,1:T(1,128)S(1)} %bitcast.28, f32[2048,2048]{1,0:T(8,128)} %copy-done), kind=kOutput, calls=%fused_computation.8 | convolution fusion | flops 54525952 | bytes 16793600 | tf_op jit(solution)/shard_map/dot_general | solution.py:32
  364.5 6.1 psum.59
  370.7 12.9 %fusion.6 = f32[1,2048]{1,0:T(1,128)S(1)} fusion(f32[2048,1]{0,1:T(1,128)S(1)} %bitcast.29, f32[2048,2048]{1,0:T(8,128)} %copy-done), kind=kOutput, calls=%fused_computation.7 | convolution fusion | flops 54525952 | bytes 16793600 | tf_op jit(solution)/shard_map/dot_general | solution.py:29
  383.5 128.0 %psum.60 = f32[2048]{0:T(1024)S(1)} all-reduce(f32[2048]{0:T(1024)S(1)} %bitcast.30), channel_id=1, replica_groups=mesh['rows'=64,'cols'=4] {'rows'}, use_global_device_ids=true, to_apply=%region_6.0 | all-reduce | flops 2048 | bytes 16384 | tf_op jit(solution)/shard_map/psum | solution.py:30
  511.6 19.6 %fusion = f32[1,2048]{1,0:T(1,128)S(1)} fusion(f32[2048,1]{0,1:T(1,128)S(1)} %bitcast.19, f32[2048,2048]{1,0:T(8,128)} %copy-done), kind=kOutput, calls=%fused_computation | convolution fusion | flops 58720256 | bytes 16793600 | tf_op jit(solution)/shard_map/dot_general | solution.py:36
  531.1 19.4 %fusion.5 = f32[1,2048]{1,0:T(1,128)S(1)} fusion(f32[2048,1]{0,1:T(1,128)S(1)} %bitcast.20, f32[2048,2048]{1,0:T(8,128)} %copy-done), kind=kOutput, calls=%fused_computation.6 | convolution fusion | flops 54525952 | bytes 16793600 | tf_op jit(solution)/shard_map/dot_general | solution.py:32
  550.5 12.8 %all-reduce = (f32[2048]{0:T(1024)S(1)}, f32[2048]{0:T(1024)S(1)}) all-reduce(f32[2048]{0:T(1024)S(1)} %bitcast.22, f32[2048]{0:T(1024)S(1)} %bitcast.21), channel_id=1, replica_groups=mesh['rows'=64,'cols'=4] {'cols'}, use_global_device_ids=true, to_apply=%region_7.0 | all-reduce | flops 4096 | bytes 32768 | tf_op jit(solution)/shard_map/psum | solution.py:37
  563.3 0.6 fusion.38
  563.9 32.5 %fusion.2 = f32[2048,128]{1,0:T(8,128)} fusion(f32[2048,2048]{1,0:T(8,128)} %copy-done, f32[2048]{0:T(1024)S(1)} %get-tuple-element.5, f32[2048]{0:T(1024)S(1)} %broadcast_divide_fusion.3, f32[2048,128]{1,0:T(8,128)S(1)} %copy-done.1, f32[2048]{0:T(1024)S(1)} %get-tuple-element.7), kind=kOutput, calls=%fused_computation.2 | convolution fusion | flops 6455296000 | bytes 18898944 | tf_op jit(solution)/shard_map/dot_general | solution.py:42
  596.4 0.0 all-reduce.3.cloned.1.call-update
  596.5 179.1 %all-reduce.3.cloned.1.call-done = f32[2048,128]{1,0:T(8,128)} async-done(((f32[2048,128]{1,0:T(8,128)}), f32[2048,128]{1,0:T(8,128)}) %all-reduce.3.cloned.1.call-update) | async-done | bytes 1048592 | tf_op jit(solution)/shard_map/psum | solution.py:45
  775.6 1.6 multiply_reduce_fusion
  777.2 2.5 broadcast_multiply_fusion
  (10 shorter events, 0.1 us)
Async XLA Ops:
  7.2 768.4 %all-reduce.3.cloned.1.call-start = ((), (), s32[]{:S(2)}) async-start(), calls=%async_computation | async-start | bytes 2097152 | tf_op jit(solution)/shard_map/psum | solution.py:45
  26.4 5.7 copy-start
  531.1 32.8 %copy-start.1 = (f32[2048,128]{1,0:T(8,128)S(1)}, f32[2048,128]{1,0:T(8,128)}, u32[]{:S(2)}) copy-start(f32[2048,128]{1,0:T(8,128)} %param.2) | copy-start | bytes 3145732
Sparse Core Ops, SparseCore 0:
  596.6 178.9 all-reduce.2
where the time goes:
time: 796 us; the launch traced here: 787 us
  blocking collectives  419 us (53%)
  waiting for transfers between devices  179 us (22%)
  matrix products  161 us (20%)
  between operations  14.4 us (2%)
    psum x3, blocking collectives, local(): col_mass = lax.psum(partial_value, 'rows')  391 us
    psum x1, waiting for transfers between devices, local(): total = lax.psum(sums, 'rows')  179 us
    dot_general x3, matrix products, local(): row_part = jnp.dot(expo, col_scale, precision=lax.Precision.HIGHEST)  57.6 us
    dot_general x3, matrix products, local(): partial_value = jnp.dot(row_scale, expo, precision=lax.Precision.HIGHEST)  35.3 us
    dot_general x1, matrix products, local(): jnp.dot(weights.T, unit_x, precision=lax.Precision.HIGHEST, preferred_ele...  32.5 us
    dot_general x1, matrix products, local(): jnp.dot(expo * scores, col_scale, precision=lax.Precision.HIGHEST)  19.6 us
    dot_general x1, matrix products, local(): jnp.dot(unit_x, unit_c.T, precision=lax.Precision.HIGHEST, preferred_elem...  16 us
  transfers between devices with their start and end apart: 1, of which 1 were waited for; matrix products, arithmetic and copies ran while one was open for 0% of the time, Pallas kernels for 0%

commit v1 on v0

v1 whole, which is shorter than its diff:
```python
import functools

import jax
import jax.numpy as jnp
from jax import lax
from jax.experimental import pallas as pl
from jax.experimental.pallas import tpu as pltpu
from jax.sharding import PartitionSpec as P

ITERS = 3
INV_TEMP = 20.0
EPS = 1e-06
F32 = jnp.float32
BF16 = jnp.bfloat16
MESH = pl.DeviceIdType.MESH
CHIPS_X, CHIPS_Z, CHIPS_Y = 4, 8, 4


def split(value):
    hi = value.astype(BF16)
    lo = (value - hi.astype(F32)).astype(BF16)
    return hi, lo


def unit_rows(value):
    return value * lax.rsqrt(jnp.sum(value * value, axis=-1, keepdims=True) + EPS)


def to_sublanes(row, width=128):
    return jnp.broadcast_to(row, (width, 128)).T


def kernel(dims, mol_count, clu_count, x_ref, c_ref, out_ref, sim_ref, e_ref, t_ref, cc_ref, xc_ref, xu_ref,
           acc_ref, csb_ref, a_buf, z_buf, y_buf, l_buf, part_ref, core_buf, xr_buf, zs_buf, zr_buf,
           a_sem, z_sem, y_sem, l_sem, core_sem, xr_sem, zr_sem, gz_sem, gx_sem, gc_sem):
    nx, nz, ny = dims
    na = 2 * nx
    mols, clus = x_ref.shape[0], c_ref.shape[0]
    rows, y = lax.axis_index("rows"), lax.axis_index("cols")
    core = lax.rem(rows, 2)
    z = lax.rem(lax.div(rows, 2), nz)
    x = lax.div(rows, 2 * nz)
    a = x * 2 + core
    other = 1 - core

    def dev(x_at, z_at, core_at):
        return ((x_at * nz + z_at) * 2 + core_at, y)

    def dev_a(k):
        return dev(lax.div(k, 2), z, lax.rem(k, 2))

    def dev_z(k):
        return dev(x, k, core)

    def dev_x(k):
        return dev(k, z, core)

    def dev_y(k):
        return (rows, k)

    barrier = pltpu.get_barrier_semaphore()
    for me, n, at in ((a, na, dev_a), (z, nz, dev_z), (y, ny, dev_y)):
        for d in range(1, n):
            pl.semaphore_signal(barrier, inc=1, device_id=at(lax.rem(me + d, n)), device_id_type=MESH)

    step_p = min(256, mols)

    def prep(i, _):
        r = pl.ds(pl.multiple_of(i * step_p, step_p), step_p)
        hi, lo = split(unit_rows(c_ref[r, :]) * INV_TEMP)
        cc_ref[r, :] = jnp.concatenate([hi, lo, hi, lo], axis=1)
        u = unit_rows(x_ref[r, :])
        xu_ref[r, :] = u
        hi, lo = split(u)
        xc_ref[r, :] = jnp.concatenate([hi, hi, lo, lo], axis=1)
        return 0

    lax.fori_loop(0, mols // step_p, prep, 0)

    row_b, col_b = min(512, clus), min(512, mols)

    def score(i, _):
        r = pl.ds(pl.multiple_of(i * row_b, row_b), row_b)
        total = None
        for j in range(mols // col_b):
            m = pl.ds(j * col_b, col_b)
            t = lax.dot_general(cc_ref[r, :], xc_ref[m, :], (((1,), (1,)), ((), ())), preferred_element_type=F32)
            e = jnp.exp(t)
            t_ref[r, m] = t
            e_ref[r, m] = e
            part = e[:, 0:128]
            for k in range(1, col_b // 128):
                part = part + e[:, 128 * k:128 * (k + 1)]
            total = part if total is None else total + part
        acc_ref[r, :] = total
        return 0

    lax.fori_loop(0, clus // row_b, score, 0)

    pl.semaphore_wait(barrier, na + nz + ny - 3)

    sends = []

    def exchange(buf, sem, it, me, n, at):
        for d in range(1, n):
            k = lax.rem(me + d, n)
            copy = pltpu.make_async_remote_copy(
                src_ref=buf.at[it, me], dst_ref=buf.at[it, me], send_sem=sem.at[0, it, k], recv_sem=sem.at[1, it, me],
                device_id=at(k), device_id_type=MESH)
            copy.start()
            sends.append(copy)
        for d in range(1, n):
            k = lax.rem(me + n - d, n)
            pltpu.make_async_remote_copy(
                src_ref=buf.at[it, k], dst_ref=buf.at[it, k], send_sem=sem.at[0, it, k], recv_sem=sem.at[1, it, k],
                device_id=at(k), device_id_type=MESH).wait_recv()
        total = buf[it, 0]
        for k in range(1, n):
            total = total + buf[it, k]
        return total

    step_r = min(64, clus)

    for it in range(ITERS):
        if it > 0:
            scale = jnp.broadcast_to(1.0 / mol_count / row_sum, (8, mols))

            def col_pass(i, scale):
                for g in range(step_r // 8):
                    r = pl.ds(pl.multiple_of(i * step_r + g * 8, 8), 8)
                    p = e_ref[r, :] * scale
                    s = p[:, 0:128]
                    for k in range(1, mols // 128):
                        s = s + p[:, 128 * k:128 * (k + 1)]
                    acc_ref[r, :] = s
                return scale

            lax.fori_loop(0, clus // step_r, col_pass, scale)
        for j in range(clus // 128):
            s = slice(128 * j, 128 * (j + 1))
            a_buf[it, a, :, s] = jnp.sum(acc_ref[s, :].T, axis=0, keepdims=True)
        z_buf[it, z] = exchange(a_buf, a_sem, it, a, na, dev_a)
        col_mass = exchange(z_buf, z_sem, it, z, nz, dev_z)
        col_scale = 1.0 / clu_count / col_mass
        for j in range(clus // 128):
            s = slice(128 * j, 128 * (j + 1))
            csb_ref[s, :] = to_sublanes(col_scale[:, s])

        last = it == ITERS - 1

        def row_pass(i, carry):
            acc, num = carry
            for g in range(step_r // 8):
                r = pl.ds(pl.multiple_of(i * step_r + g * 8, 8), 8)
                w = e_ref[r, :] * jnp.concatenate([csb_ref[r, :]] * (mols // 128), axis=1)
                acc = acc + w
                if last:
                    num = num + w * t_ref[r, :]
            return acc, num

        zero = jnp.zeros((8, mols), F32)
        acc, num = lax.fori_loop(0, clus // step_r, row_pass, (zero, zero if last else jnp.zeros((8, 128), F32)))
        row_part = jnp.sum(acc, axis=0, keepdims=True)
        if last:
            l_buf[0, y, 0:1, :] = row_part
            l_buf[0, y, 1:2, :] = jnp.sum(num, axis=0, keepdims=True)
            both = exchange(l_buf, l_sem, 0, y, ny, dev_y)
            row_sum, numer = both[0:1, :], both[1:2, :]
        else:
            y_buf[it, y] = row_part
            row_sum = exchange(y_buf, y_sem, it, y, ny, dev_y)

    sim_ref[...] = numer / row_sum * (1.0 / INV_TEMP)

    inv = 1.0 / row_sum
    for j in range(mols // 128):
        s = slice(128 * j, 128 * (j + 1))
        hi, lo = split(xu_ref[s, :] * to_sublanes(inv[:, s]))
        xc_ref[s, 0:256] = jnp.concatenate([hi, lo], axis=1)

    blk = clus // na
    sub = blk // nz

    def block_rows(b):
        return pl.ds(pl.multiple_of(b * blk, blk), blk)

    def sums(b):
        r = block_rows(b)
        hi, lo = split(e_ref[r, :])
        p = jnp.dot(jnp.concatenate([hi, lo], axis=0), xc_ref[:, 0:256], preferred_element_type=F32)
        p = p[:, 0:128] + p[:, 128:256]
        return (p[0:blk] + p[blk:2 * blk]) * csb_ref[r, :]

    def remote(src, dst, send, recv, to):
        return pltpu.make_async_remote_copy(
            src_ref=src, dst_ref=dst, send_sem=send, recv_sem=recv, device_id=to, device_id_type=MESH)

    def to_core(q):
        b = other * nx + lax.rem(x + 1 + q, nx)
        return remote(part_ref.at[block_rows(b)], core_buf.at[q], core_sem.at[0, q], core_sem.at[1, q],
                      dev(x, z, other))

    def to_x(q):
        j = lax.rem(x + 1 + q, nx)
        return remote(part_ref.at[block_rows(core * nx + j)], xr_buf.at[x], xr_sem.at[0, j], xr_sem.at[1, x],
                      dev_x(j))

    def other_half(q, _):
        b = other * nx + lax.rem(x + 1 + q, nx)
        part_ref[block_rows(b), :] = sums(b)
        to_core(q).start()
        return 0

    lax.fori_loop(0, nx, other_half, 0)

    def own_half(q, _):
        j = lax.rem(x + 1 + q, nx)
        b = core * nx + j
        v = sums(b)
        to_core(q).wait_recv()
        v = v + core_buf[q]

        @pl.when(q < nx - 1)
        def _():
            part_ref[block_rows(b), :] = v
            to_x(q).start()

        @pl.when(q == nx - 1)
        def _():
            xr_buf[x] = v

        return 0

    lax.fori_loop(0, nx, own_half, 0)
    for d in range(1, nx):
        k = lax.rem(x + d, nx)
        remote(xr_buf.at[k], xr_buf.at[k], xr_sem.at[0, k], xr_sem.at[1, k], dev_x(k)).wait_recv()
    total = xr_buf[0]
    for k in range(1, nx):
        total = total + xr_buf[k]
    zs_buf[...] = total

    def sub_rows(k):
        return pl.ds(pl.multiple_of(k * sub, sub), sub)

    for d in range(1, nz):
        k = lax.rem(z + d, nz)
        copy = remote(zs_buf.at[sub_rows(k)], zr_buf.at[z], zr_sem.at[0, k], zr_sem.at[1, z], dev_z(k))
        copy.start()
        sends.append(copy)
    zr_buf[z] = zs_buf[sub_rows(z), :]
    for d in range(1, nz):
        k = lax.rem(z + nz - d, nz)
        remote(zr_buf.at[k], zr_buf.at[k], zr_sem.at[0, k], zr_sem.at[1, k], dev_z(k)).wait_recv()
    total = zr_buf[0]
    for k in range(1, nz):
        total = total + zr_buf[k]

    mine = core * nx + x

    def out_sub(k):
        return out_ref.at[pl.ds(pl.multiple_of(mine * blk + k * sub, sub), sub)]

    out_ref[pl.ds(pl.multiple_of(mine * blk + z * sub, sub), sub), :] = unit_rows(total)
    for d in range(1, nz):
        k = lax.rem(z + d, nz)
        copy = remote(out_sub(z), out_sub(z), gz_sem.at[0, k], gz_sem.at[1, z], dev_z(k))
        copy.start()
        sends.append(copy)
    for d in range(1, nz):
        k = lax.rem(z + nz - d, nz)
        remote(out_sub(k), out_sub(k), gz_sem.at[0, k], gz_sem.at[1, k], dev_z(k)).wait_recv()

    def out_blk(b):
        return out_ref.at[block_rows(b)]

    def forward(k):
        copy = remote(out_blk(core * nx + k), out_blk(core * nx + k), gc_sem.at[0, k], gc_sem.at[1, k],
                      dev(x, z, other))
        copy.start()
        sends.append(copy)

    for d in range(1, nx):
        k = lax.rem(x + d, nx)
        copy = remote(out_blk(mine), out_blk(mine), gx_sem.at[0, k], gx_sem.at[1, x], dev_x(k))
        copy.start()
        sends.append(copy)
    forward(x)
    for d in (1, 3, 2) if nx == 4 else range(1, nx):
        k = lax.rem(x + d, nx)
        remote(out_blk(core * nx + k), out_blk(core * nx + k), gx_sem.at[0, k], gx_sem.at[1, k],
               dev_x(k)).wait_recv()
        forward(k)
    for k in range(nx):
        b = other * nx + k
        remote(out_blk(b), out_blk(b), gc_sem.at[0, k], gc_sem.at[1, k], dev(x, z, other)).wait_recv()
    for copy in sends:
        copy.wait_send()
    for q in range(nx):
        to_core(q).wait_send()
        if q < nx - 1:
            to_x(q).wait_send()


def local(dims, embeddings, centres):
    nx, nz, ny = dims
    na = 2 * nx
    mols, emb = embeddings.shape
    clus = centres.shape[0]
    blk = clus // na
    sub = blk // nz
    dma = pltpu.SemaphoreType.DMA
    new_centres, expected = pl.pallas_call(
        functools.partial(kernel, dims, mols * lax.axis_size("rows"), clus * lax.axis_size("cols")),
        out_shape=(jax.ShapeDtypeStruct((clus, emb), F32), jax.ShapeDtypeStruct((1, mols), F32)),
        in_specs=[pl.BlockSpec(memory_space=pltpu.VMEM)] * 2,
        out_specs=(pl.BlockSpec(memory_space=pltpu.VMEM),) * 2,
        scratch_shapes=[
            pltpu.VMEM((clus, mols), F32),
            pltpu.VMEM((clus, mols), F32),
            pltpu.VMEM((clus, 4 * emb), BF16),
            pltpu.VMEM((mols, 4 * emb), BF16),
            pltpu.VMEM((mols, emb), F32),
            pltpu.VMEM((clus, 128), F32),
            pltpu.VMEM((clus, 128), F32),
            pltpu.VMEM((ITERS, na, 1, clus), F32),
            pltpu.VMEM((ITERS, nz, 1, clus), F32),
            pltpu.VMEM((ITERS - 1, ny, 1, mols), F32),
            pltpu.VMEM((1, ny, 2, mols), F32),
            pltpu.VMEM((clus, emb), F32),
            pltpu.VMEM((nx, blk, emb), F32),
            pltpu.VMEM((nx, blk, emb), F32),
            pltpu.VMEM((blk, emb), F32),
            pltpu.VMEM((nz, sub, emb), F32),
            dma((2, ITERS, na)),
            dma((2, ITERS, nz)),
            dma((2, ITERS - 1, ny)),
            dma((2, 1, ny)),
            dma((2, nx)),
            dma((2, nx)),
            dma((2, nz)),
            dma((2, nz)),
            dma((2, nx)),
            dma((2, nx)),
        ],
        compiler_params=pltpu.CompilerParams(
            collective_id=0, has_side_effects=True, vmem_limit_bytes=60 * 1024 * 1024),
        cost_estimate=pl.CostEstimate(flops=2 * 8 * mols * clus * emb, bytes_accessed=4 * 1024 * 1024,
                                      transcendentals=mols * clus),
    )(embeddings, centres)
    return new_centres, expected.reshape(mols)


def solution(mesh, dims=(CHIPS_X, CHIPS_Z, CHIPS_Y)):
    return jax.shard_map(
        functools.partial(local, dims), mesh=mesh, in_specs=(P("rows", None), P("cols", None)),
        out_specs=(P("cols", None), P("rows")), check_vma=False)
```

time: 796 us -> 101 us (0.13); the launches traced: 787 us -> 101 us
  blocking collectives: 419 us -> 0 us
  waiting for transfers between devices: 179 us -> 0 us
  matrix products: 161 us -> 0 us
  Pallas kernels: 0 us -> 97.3 us
  between operations: 14.4 us -> 0.65 us
    psum x6 -> x0, blocking collectives: 419 us -> none  [the longest x3 391 us: local(): col_mass = lax.psum(partial_value, 'rows')]
    psum x1 -> x0, waiting for transfers between devices: 179 us -> none  [local(): total = lax.psum(sums, 'rows')]
    dot_general x9 -> x0, matrix products: 161 us -> none  [the longest x3 57.6 us: local(): row_part = jnp.dot(expo, col_scale, precision=lax.Precision.HIGHEST)]
    pallas_call x0 -> x1, Pallas kernels: none -> 97.3 us  [local(): pl.pallas_call(functools.partial(kernel, dims, mols * lax.axis_size('rows...]
  transfers between devices with their start and end apart: 1 -> 0, of which waited for: 1 -> 0; matrix products, arithmetic and copies ran while one was open for 0% -> 0% of each run, Pallas kernels for 0% -> 0%
where the time goes in v1:
time: 101 us
  Pallas kernels  97.3 us (96%)
  local copies, waits for them, and re-layouts  2.87 us (3%)
    pallas_call x1, Pallas kernels, local(): pl.pallas_call(functools.partial(kernel, dims, mols * lax.axis_size('rows...  97.3 us
    unnamed x4, local copies, waits for them, and re-layouts  2.87 us

profile of v1, /device:TPU:1, one launch (start us, length us, event | category | flops | bytes accessed | tf_op | source)
XLA Modules:
  0.0 100.8 jit_solution(12126752564458480083)
XLA Ops:
  0.6 97.3 %shard_map.41 = (f32[2048,128]{1,0:T(8,128)}, f32[1,2048]{1,0:T(1,128)}) custom-call(f32[2048,128]{1,0:T(8,128)} %x_ref.1, f32[2048,128]{1,0:T(8,128)} %c_ref.1), custom_call_target="tpu_custom_call" | custom-call | flops 8589934592 | bytes 4194304 | tf_op jit(solution)/shard_map/pallas_call | solution.py:313
  98.0 0.0 copy-start
  98.0 2.3 %copy.6 = f32[2048,128]{1,0:T(8,128)} copy(f32[2048,128]{1,0:T(8,128)} %get-tuple-element.8) | data formatting | bytes 2097152
  100.2 0.0 copy-done
  100.2 0.6 copy.7
Async XLA Ops:
  98.0 2.3 %copy-start = (f32[1,2048]{1,0:T(1,128)S(1)}, f32[1,2048]{1,0:T(1,128)}, u32[]{:S(2)}) copy-start(f32[1,2048]{1,0:T(1,128)} %get-tuple-element.5) | copy-start | bytes 24580

commit v2 on v0

v2 whole, which is shorter than its diff:
```python
import functools

import jax
import jax.numpy as jnp
from jax import lax
from jax.experimental import pallas as pl
from jax.experimental.pallas import tpu as pltpu
from jax.sharding import PartitionSpec as P

ITERS = 3
INV_TEMP = 20.0
EPS = 1e-06
F32 = jnp.float32
BF16 = jnp.bfloat16
MESH = pl.DeviceIdType.MESH
CHIPS_X, CHIPS_Z, CHIPS_Y = 4, 8, 4
CHUNKS = 4


def split(value):
    hi = value.astype(BF16)
    lo = (value - hi.astype(F32)).astype(BF16)
    return hi, lo


def unit_rows(value):
    return value * lax.rsqrt(jnp.sum(value * value, axis=-1, keepdims=True) + EPS)


def to_sublanes(row, width=128):
    return jnp.broadcast_to(row, (width, 128)).T


def kernel(dims, mol_count, clu_count, x_ref, c_ref, out_ref, sim_ref, e_ref, t_ref, cc_ref, xc_ref, xu_ref,
           acc_ref, csb_ref, half_buf, a_buf, cs_buf, y_buf, core_buf, send_buf, xr_buf, zs_buf, zr_buf,
           half_sem, a_sem, cs_sem, y_sem, core_sem, xr_sem, zr_sem, gz_sem, gx_sem, gc_sem):
    nx, nz, ny = dims
    mols, clus = x_ref.shape[0], c_ref.shape[0]
    half = clus // 2
    lanes = half // 128
    rows, y = lax.axis_index("rows"), lax.axis_index("cols")
    core = lax.rem(rows, 2)
    z = lax.rem(lax.div(rows, 2), nz)
    x = lax.div(rows, 2 * nz)
    chip = x * nz + z
    other = 1 - core

    def dev(x_at, z_at, core_at):
        return ((x_at * nz + z_at) * 2 + core_at, y)

    def dev_y(k):
        return (rows, k)

    twin = dev(x, z, other)
    away = [(dx, dz) for dx in range(nx) for dz in range(nz) if dx or dz]
    away.sort(key=lambda p: -(min(p[0], nx - p[0]) + min(p[1], nz - p[1])))

    def chip_at(p):
        return lax.rem(x + p[0], nx), lax.rem(z + p[1], nz)

    def near(n):
        return sorted(range(1, n), key=lambda d: -min(d, n - d))

    barrier = pltpu.get_barrier_semaphore()
    pl.semaphore_signal(barrier, inc=1, device_id=twin, device_id_type=MESH)
    for p in away:
        pl.semaphore_signal(barrier, inc=1, device_id=dev(*chip_at(p), core), device_id_type=MESH)
    for d in range(1, ny):
        pl.semaphore_signal(barrier, inc=1, device_id=dev_y(lax.rem(y + d, ny)), device_id_type=MESH)

    def remote(src, dst, send, recv, to):
        return pltpu.make_async_remote_copy(
            src_ref=src, dst_ref=dst, send_sem=send, recv_sem=recv, device_id=to, device_id_type=MESH)

    sent = []

    def start(src, dst, sem, to, keep=True):
        copy = remote(src, dst, sem.at[0], sem.at[1], to)
        copy.start()
        if keep:
            sent.append((src, sem))

    def wait(ref, sem):
        remote(ref, ref, sem.at[0], sem.at[1], twin).wait_recv()

    def at(start_row, size):
        return pl.ds(pl.multiple_of(start_row, size), size)

    step_p = min(256, mols)

    def prep(i, _):
        r = at(i * step_p, step_p)
        hi, lo = split(unit_rows(c_ref[r, :]) * INV_TEMP)
        cc_ref[r, :] = jnp.concatenate([hi, lo, hi, lo], axis=1)
        u = unit_rows(x_ref[r, :])
        xu_ref[r, :] = u
        hi, lo = split(u)
        xc_ref[r, :] = jnp.concatenate([hi, hi, lo, lo], axis=1)
        return 0

    lax.fori_loop(0, mols // step_p, prep, 0)

    row_b, col_b = min(512, clus), min(512, mols)

    def score(i, _):
        r = at(i * row_b, row_b)
        total = None
        for j in range(mols // col_b):
            m = pl.ds(j * col_b, col_b)
            t = lax.dot_general(cc_ref[r, :], xc_ref[m, :], (((1,), (1,)), ((), ())), preferred_element_type=F32)
            e = jnp.exp(t)
            t_ref[r, m] = t
            e_ref[r, m] = e
            part = e[:, 0:128]
            for k in range(1, col_b // 128):
                part = part + e[:, 128 * k:128 * (k + 1)]
            total = part if total is None else total + part
        acc_ref[r, :] = total
        return 0

    lax.fori_loop(0, clus // row_b, score, 0)

    step_r = min(64, half)
    steps = half // step_r
    zero = jnp.zeros((8, mols), F32)

    def col_pass(of, scale):
        def body(i, scale):
            for g in range(step_r // 8):
                r = at(of * half + i * step_r + g * 8, 8)
                p = e_ref[r, :] * scale
                s = p[:, 0:128]
                for k in range(1, mols // 128):
                    s = s + p[:, 128 * k:128 * (k + 1)]
                acc_ref[r, :] = s
            return scale

        lax.fori_loop(0, steps, body, scale)

    def col_vec(of, dst):
        for j in range(lanes):
            dst[j:j + 1, :] = jnp.sum(acc_ref[at(of * half + 128 * j, 128), :].T, axis=0, keepdims=True)

    def spread(of, src):
        for j in range(lanes):
            csb_ref[at(of * half + 128 * j, 128), :] = to_sublanes(src[j:j + 1, :])

    def scaled(r):
        return e_ref[r, :] * jnp.concatenate([csb_ref[r, :]] * (mols // 128), axis=1)

    def row_pass(of, acc):
        def body(i, acc):
            for g in range(step_r // 8):
                acc = acc + scaled(at(of * half + i * step_r + g * 8, 8))
            return acc

        return lax.fori_loop(0, steps, body, acc)

    def sum_cols(slot, value):
        y_buf[slot, y] = value
        for d in near(ny):
            k = lax.rem(y + d, ny)
            start(y_buf.at[slot, y], y_buf.at[slot, y], y_sem.at[slot], dev_y(k))

        def result():
            wait(y_buf.at[slot, pl.ds(0, ny - 1)], y_sem.at[slot])
            total = y_buf[slot, 0]
            for k in range(1, ny):
                total = total + y_buf[slot, k]
            return total

        return result

    for it in range(ITERS):
        if it > 0:
            scale = jnp.broadcast_to(1.0 / mol_count / row_sum, (8, mols))
            col_pass(other, scale)
        else:
            pl.semaphore_wait(barrier, nx * nz + ny - 1)
        col_vec(other, half_buf.at[it, 0])
        start(half_buf.at[it, 0], half_buf.at[it, 1], half_sem.at[it], twin)
        if it > 0:
            col_pass(core, scale)
        mine = a_buf.at[it, chip]
        col_vec(core, mine)
        wait(half_buf.at[it, 1], half_sem.at[it])
        mine[...] = mine[...] + half_buf[it, 1]
        for p in away:
            start(mine, mine, a_sem.at[it], dev(*chip_at(p), core))
        wait(a_buf.at[it, pl.ds(0, nx * nz - 1)], a_sem.at[it])
        col_mass = jnp.sum(a_buf[it], axis=0)
        cs_buf[it, core] = 1.0 / clu_count / col_mass
        start(cs_buf.at[it, core], cs_buf.at[it, core], cs_sem.at[it], twin)
        spread(core, cs_buf.at[it, core])
        acc = row_pass(core, zero)
        wait(cs_buf.at[it, other], cs_sem.at[it])
        spread(other, cs_buf.at[it, other])
        acc = row_pass(other, acc)
        row_sum = sum_cols(it, jnp.sum(acc, axis=0, keepdims=True))()

    inv = 1.0 / row_sum
    for j in range(mols // 128):
        s = slice(128 * j, 128 * (j + 1))
        hi, lo = split(xu_ref[s, :] * to_sublanes(inv[:, s]))
        xc_ref[s, 0:256] = jnp.concatenate([hi, lo], axis=1)

    size = clus // CHUNKS
    part = size // 2
    blk = part // nx
    sub = blk // nz

    def row_at(k, core_at, x_at=0, z_at=0):
        return k * size + core_at * part + x_at * blk + z_at * sub

    def sums(r):
        hi, lo = split(e_ref[r, :])
        p = jnp.dot(jnp.concatenate([hi, lo], axis=0), xc_ref[:, 0:256], preferred_element_type=F32)
        p = p[:, 0:128] + p[:, 128:256]
        return (p[0:part] + p[part:2 * part]) * csb_ref[r, :]

    def to_twin(k):
        return remote(send_buf.at[k, 1], core_buf.at[k], core_sem.at[k, 0], core_sem.at[k, 1], twin)

    def products(k, _):
        send_buf[k, 1] = sums(at(row_at(k, other), part))
        to_twin(k).start()
        send_buf[k, 0] = sums(at(row_at(k, core), part))
        to_twin(k).wait_recv()
        send_buf[k, 0] = send_buf[k, 0] + core_buf[k]
        for d in near(nx):
            to = lax.rem(x + d, nx)
            remote(send_buf.at[k, 0, at(to * blk, blk)], xr_buf.at[k, x], xr_sem.at[k, 0], xr_sem.at[k, 1],
                   dev(to, z, core)).start()
        xr_buf[k, x] = send_buf[k, 0, at(x * blk, blk), :]
        return 0

    lax.fori_loop(0, CHUNKS, products, 0)

    def after_x(k):
        wait(xr_buf.at[k, pl.ds(0, nx - 1)], xr_sem.at[k])
        total = xr_buf[k, 0]
        for j in range(1, nx):
            total = total + xr_buf[k, j]
        zs_buf[k] = total
        for d in near(nz):
            to = lax.rem(z + d, nz)
            start(zs_buf.at[k, at(to * sub, sub)], zr_buf.at[k, z], zr_sem.at[k], dev(x, to, core))
        zr_buf[k, z] = zs_buf[k, at(z * sub, sub), :]

    def after_z(k):
        wait(zr_buf.at[k, pl.ds(0, nz - 1)], zr_sem.at[k])
        total = zr_buf[k, 0]
        for j in range(1, nz):
            total = total + zr_buf[k, j]
        r = at(row_at(k, core, x, z), sub)
        out_ref[r, :] = unit_rows(total)
        for d in near(nz):
            to = lax.rem(z + d, nz)
            start(out_ref.at[r], out_ref.at[r], gz_sem.at[k], dev(x, to, core))

    def forward(k, x_at):
        ref = out_ref.at[at(row_at(k, core, x_at), blk)]
        start(ref, ref, gc_sem.at[k], twin)

    def after_gather_z(k):
        wait(zr_buf.at[k, pl.ds(0, nz - 1)], gz_sem.at[k])
        ref = out_ref.at[at(row_at(k, core, x), blk)]
        for d in near(nx):
            to = lax.rem(x + d, nx)
            start(ref, ref, gx_sem.at[k], dev(to, z, core))
        forward(k, x)

    def after_gather_x(k):
        wait(xr_buf.at[k, pl.ds(0, nx - 1)], gx_sem.at[k])
        for d in range(1, nx):
            forward(k, lax.rem(x + d, nx))

    for k in range(CHUNKS):
        after_x(k)

    def numer_pass(i, acc):
        for g in range(step_r // 8):
            r = at(i * step_r + g * 8, 8)
            acc = acc + scaled(r) * t_ref[r, :]
        return acc

    numer = jnp.sum(lax.fori_loop(0, 2 * steps, numer_pass, zero), axis=0, keepdims=True)
    numer = sum_cols(ITERS, numer)
    for k in range(CHUNKS):
        after_z(k)
    sim_ref[...] = numer() / row_sum * (1.0 / INV_TEMP)
    for k in range(CHUNKS):
        after_gather_z(k)
    for k in range(CHUNKS):
        after_gather_x(k)
    for k in range(CHUNKS):
        wait(core_buf.at[k], gc_sem.at[k])

    for src, sem in sent:
        remote(src, src, sem.at[0], sem.at[1], twin).wait_send()
    for k in range(CHUNKS):
        to_twin(k).wait_send()
        for d in range(1, nx):
            remote(xr_buf.at[k, 0], xr_buf.at[k, 0], xr_sem.at[k, 0], xr_sem.at[k, 1], twin).wait_send()


def local(dims, embeddings, centres):
    nx, nz, ny = dims
    mols, emb = embeddings.shape
    clus = centres.shape[0]
    half = clus // 2
    size = clus // CHUNKS
    part = size // 2
    blk = part // nx
    sub = blk // nz
    dma = pltpu.SemaphoreType.DMA
    new_centres, expected = pl.pallas_call(
        functools.partial(kernel, dims, mols * lax.axis_size("rows"), clus * lax.axis_size("cols")),
        out_shape=(jax.ShapeDtypeStruct((clus, emb), F32), jax.ShapeDtypeStruct((1, mols), F32)),
        in_specs=[pl.BlockSpec(memory_space=pltpu.VMEM)] * 2,
        out_specs=(pl.BlockSpec(memory_space=pltpu.VMEM),) * 2,
        scratch_shapes=[
            pltpu.VMEM((clus, mols), F32),
            pltpu.VMEM((clus, mols), F32),
            pltpu.VMEM((clus, 4 * emb), BF16),
            pltpu.VMEM((mols, 4 * emb), BF16),
            pltpu.VMEM((mols, emb), F32),
            pltpu.VMEM((clus, 128), F32),
            pltpu.VMEM((clus, 128), F32),
            pltpu.VMEM((ITERS, 2, half // 128, 128), F32),
            pltpu.VMEM((ITERS, nx * nz, half // 128, 128), F32),
            pltpu.VMEM((ITERS, 2, half // 128, 128), F32),
            pltpu.VMEM((ITERS + 1, ny, 1, mols), F32),
            pltpu.VMEM((CHUNKS, part, emb), F32),
            pltpu.VMEM((CHUNKS, 2, part, emb), F32),
            pltpu.VMEM((CHUNKS, nx, blk, emb), F32),
            pltpu.VMEM((CHUNKS, blk, emb), F32),
            pltpu.VMEM((CHUNKS, nz, sub, emb), F32),
            dma((ITERS, 2)),
            dma((ITERS, 2)),
            dma((ITERS, 2)),
            dma((ITERS + 1, 2)),
            dma((CHUNKS, 2)),
            dma((CHUNKS, 2)),
            dma((CHUNKS, 2)),
            dma((CHUNKS, 2)),
            dma((CHUNKS, 2)),
            dma((CHUNKS, 2)),
        ],
        compiler_params=pltpu.CompilerParams(
            collective_id=0, has_side_effects=True, vmem_limit_bytes=60 * 1024 * 1024),
        cost_estimate=pl.CostEstimate(flops=2 * 8 * mols * clus * emb, bytes_accessed=4 * 1024 * 1024,
                                      transcendentals=mols * clus),
    )(embeddings, centres)
    return new_centres, expected.reshape(mols)


def solution(mesh, dims=(CHIPS_X, CHIPS_Z, CHIPS_Y)):
    return jax.shard_map(
        functools.partial(local, dims), mesh=mesh, in_specs=(P("rows", None), P("cols", None)),
        out_specs=(P("cols", None), P("rows")), check_vma=False)
```

time: 796 us -> 90.3 us (0.11); the launches traced: 787 us -> 90.2 us
  blocking collectives: 419 us -> 0 us
  waiting for transfers between devices: 179 us -> 0 us
  matrix products: 161 us -> 0 us
  Pallas kernels: 0 us -> 86.7 us
  between operations: 14.4 us -> 0.65 us
    psum x6 -> x0, blocking collectives: 419 us -> none  [the longest x3 391 us: local(): col_mass = lax.psum(partial_value, 'rows')]
    psum x1 -> x0, waiting for transfers between devices: 179 us -> none  [local(): total = lax.psum(sums, 'rows')]
    dot_general x9 -> x0, matrix products: 161 us -> none  [the longest x3 57.6 us: local(): row_part = jnp.dot(expo, col_scale, precision=lax.Precision.HIGHEST)]
    pallas_call x0 -> x1, Pallas kernels: none -> 86.7 us  [local(): pl.pallas_call(functools.partial(kernel, dims, mols * lax.axis_size('rows...]
  transfers between devices with their start and end apart: 1 -> 0, of which waited for: 1 -> 0; matrix products, arithmetic and copies ran while one was open for 0% -> 0% of each run, Pallas kernels for 0% -> 0%
where the time goes in v2:
time: 90.3 us; the launch traced here: 90.2 us
  Pallas kernels  86.7 us (96%)
  local copies, waits for them, and re-layouts  2.87 us (3%)
    pallas_call x1, Pallas kernels, local(): pl.pallas_call(functools.partial(kernel, dims, mols * lax.axis_size('rows...  86.7 us
    unnamed x4, local copies, waits for them, and re-layouts  2.87 us

profile of v2, /device:TPU:1, one launch (start us, length us, event | category | flops | bytes accessed | tf_op | source)
XLA Modules:
  0.0 90.2 jit_solution(13345233465012053804)
XLA Ops:
  0.6 86.7 %shard_map.41 = (f32[2048,128]{1,0:T(8,128)}, f32[1,2048]{1,0:T(1,128)}) custom-call(f32[2048,128]{1,0:T(8,128)} %x_ref.1, f32[2048,128]{1,0:T(8,128)} %c_ref.1), custom_call_target="tpu_custom_call" | custom-call | flops 8589934592 | bytes 4194304 | tf_op jit(solution)/shard_map/pallas_call | solution.py:317
  87.3 0.0 copy-start
  87.3 2.3 %copy.6 = f32[2048,128]{1,0:T(8,128)} copy(f32[2048,128]{1,0:T(8,128)} %get-tuple-element.8) | data formatting | bytes 2097152
  89.6 0.0 copy-done
  89.6 0.6 copy.7
Async XLA Ops:
  87.3 2.3 %copy-start = (f32[1,2048]{1,0:T(1,128)S(1)}, f32[1,2048]{1,0:T(1,128)}, u32[]{:S(2)}) copy-start(f32[1,2048]{1,0:T(1,128)} %get-tuple-element.5) | copy-start | bytes 24580

commit v3 on v2

--- a/solution.py
+++ b/solution.py
@@ -15,6 +15,7 @@
 MESH = pl.DeviceIdType.MESH
 CHIPS_X, CHIPS_Z, CHIPS_Y = 4, 8, 4
 CHUNKS = 4
+Z_FIRST = (0,)
 
 
 def split(value):
@@ -31,11 +32,18 @@
     return jnp.broadcast_to(row, (width, 128)).T
 
 
-def kernel(dims, mol_count, clu_count, x_ref, c_ref, out_ref, sim_ref, e_ref, t_ref, cc_ref, xc_ref, xu_ref,
+def kernel(dims, mol_count, clu_count, x_hbm, c_hbm, out_hbm, sim_ref, out_ref, e_ref, t_ref, cc_ref, xc_ref, xu_ref,
            acc_ref, csb_ref, half_buf, a_buf, cs_buf, y_buf, core_buf, send_buf, xr_buf, zs_buf, zr_buf,
-           half_sem, a_sem, cs_sem, y_sem, core_sem, xr_sem, zr_sem, gz_sem, gx_sem, gc_sem):
+           in_sem, out_sem, half_sem, a_sem, cs_sem, y_sem, core_sem, xr_sem, zr_sem, gz_sem, gx_sem, gc_sem):
     nx, nz, ny = dims
-    mols, clus = x_ref.shape[0], c_ref.shape[0]
+    mols, clus = x_hbm.shape[0], c_hbm.shape[0]
+    step_p = min(256, mols)
+    loads = []
+    for i in range(mols // step_p):
+        r = pl.ds(i * step_p, step_p)
+        for k, (src, dst) in enumerate(((c_hbm, acc_ref), (x_hbm, xu_ref))):
+            loads.append(pltpu.make_async_copy(src.at[r], dst.at[r], in_sem.at[i, k]))
+            loads[-1].start()
     half = clus // 2
     lanes = half // 128
     rows, y = lax.axis_index("rows"), lax.axis_index("cols")
@@ -86,28 +94,26 @@
     def at(start_row, size):
         return pl.ds(pl.multiple_of(start_row, size), size)
 
-    step_p = min(256, mols)
-
-    def prep(i, _):
-        r = at(i * step_p, step_p)
-        hi, lo = split(unit_rows(c_ref[r, :]) * INV_TEMP)
-        cc_ref[r, :] = jnp.concatenate([hi, lo, hi, lo], axis=1)
-        u = unit_rows(x_ref[r, :])
+    for i in range(mols // step_p):
+        r = pl.ds(i * step_p, step_p)
+        loads[2 * i].wait()
+        cc_ref[r, :] = jnp.concatenate(split(unit_rows(acc_ref[r, :]) * INV_TEMP), axis=1)
+        loads[2 * i + 1].wait()
+        u = unit_rows(xu_ref[r, :])
         xu_ref[r, :] = u
-        hi, lo = split(u)
-        xc_ref[r, :] = jnp.concatenate([hi, hi, lo, lo], axis=1)
-        return 0
-
-    lax.fori_loop(0, mols // step_p, prep, 0)
-
-    row_b, col_b = min(512, clus), min(512, mols)
+        xc_ref[r, :] = jnp.concatenate(split(u), axis=1)
+
+    row_b, col_b = min(1024, clus), min(256, mols)
 
     def score(i, _):
         r = at(i * row_b, row_b)
         total = None
         for j in range(mols // col_b):
             m = pl.ds(j * col_b, col_b)
-            t = lax.dot_general(cc_ref[r, :], xc_ref[m, :], (((1,), (1,)), ((), ())), preferred_element_type=F32)
+            c, u = cc_ref[r, :], xc_ref[m, :]
+            hi, lo = u[:, 0:128], u[:, 128:256]
+            t = lax.dot_general(jnp.concatenate([c, c], axis=1), jnp.concatenate([hi, hi, lo, lo], axis=1),
+                                (((1,), (1,)), ((), ())), preferred_element_type=F32)
             e = jnp.exp(t)
             t_ref[r, m] = t
             e_ref[r, m] = e
@@ -120,7 +126,7 @@
 
     lax.fori_loop(0, clus // row_b, score, 0)
 
-    step_r = min(64, half)
+    step_r = min(128, half)
     steps = half // step_r
     zero = jnp.zeros((8, mols), F32)
 
@@ -202,81 +208,115 @@
     for j in range(mols // 128):
         s = slice(128 * j, 128 * (j + 1))
         hi, lo = split(xu_ref[s, :] * to_sublanes(inv[:, s]))
-        xc_ref[s, 0:256] = jnp.concatenate([hi, lo], axis=1)
+        xc_ref[s, :] = jnp.concatenate([hi, lo], axis=1)
 
     size = clus // CHUNKS
     part = size // 2
-    blk = part // nx
-    sub = blk // nz
-
-    def row_at(k, core_at, x_at=0, z_at=0):
-        return k * size + core_at * part + x_at * blk + z_at * sub
+
+    class Axis:
+        def __init__(self, n, place, at_place):
+            self.n, self.place, self.at_place = n, place, at_place
+
+        def peers(self):
+            for d in near(self.n):
+                to = lax.rem(self.place + d, self.n)
+                yield to, self.at_place(to)
+
+    x_axis = Axis(nx, x, lambda k: dev(k, z, core))
+    z_axis = Axis(nz, z, lambda k: dev(x, k, core))
+    sub = part // (nx * nz)
+
+    def axes(k):
+        return (z_axis, x_axis) if k in Z_FIRST else (x_axis, z_axis)
+
+    def row_at(k, core_at, first=0, second=0):
+        return k * size + core_at * part + first * (part // axes(k)[0].n) + second * sub
 
     def sums(r):
-        hi, lo = split(e_ref[r, :])
-        p = jnp.dot(jnp.concatenate([hi, lo], axis=0), xc_ref[:, 0:256], preferred_element_type=F32)
+        n = r.size
+        p = jnp.dot(jnp.concatenate(split(e_ref[r, :]), axis=0), xc_ref[...], preferred_element_type=F32)
         p = p[:, 0:128] + p[:, 128:256]
-        return (p[0:part] + p[part:2 * part]) * csb_ref[r, :]
+        return (p[0:n] + p[n:2 * n]) * csb_ref[r, :]
 
     def to_twin(k):
-        return remote(send_buf.at[k, 1], core_buf.at[k], core_sem.at[k, 0], core_sem.at[k, 1], twin)
+        return remote(send_buf.at[k, other], core_buf.at[k], core_sem.at[k, 0], core_sem.at[k, 1], twin)
+
+    def scatter(k):
+        one = axes(k)[0]
+        blk = part // one.n
+        to_twin(k).wait_recv()
+        send_buf[k, core] = send_buf[k, core] + core_buf[k]
+        for to, peer in one.peers():
+            start(send_buf.at[k, core, at(to * blk, blk)], xr_buf.at[k, at(one.place * blk, blk)], xr_sem.at[k], peer,
+                  False)
+        xr_buf[k, at(one.place * blk, blk), :] = send_buf[k, core, at(one.place * blk, blk), :]
+
+    last = CHUNKS - 1
 
     def products(k, _):
-        send_buf[k, 1] = sums(at(row_at(k, other), part))
+        both = sums(at(k * size, size))
+        send_buf[k, 0] = both[0:part]
+        send_buf[k, 1] = both[part:size]
         to_twin(k).start()
-        send_buf[k, 0] = sums(at(row_at(k, core), part))
-        to_twin(k).wait_recv()
-        send_buf[k, 0] = send_buf[k, 0] + core_buf[k]
-        for d in near(nx):
-            to = lax.rem(x + d, nx)
-            remote(send_buf.at[k, 0, at(to * blk, blk)], xr_buf.at[k, x], xr_sem.at[k, 0], xr_sem.at[k, 1],
-                   dev(to, z, core)).start()
-        xr_buf[k, x] = send_buf[k, 0, at(x * blk, blk), :]
+        for done in range(last - 1):
+            @pl.when(k == done + 1)
+            def _():
+                scatter(done)
+
         return 0
 
-    lax.fori_loop(0, CHUNKS, products, 0)
-
-    def after_x(k):
-        wait(xr_buf.at[k, pl.ds(0, nx - 1)], xr_sem.at[k])
-        total = xr_buf[k, 0]
-        for j in range(1, nx):
-            total = total + xr_buf[k, j]
-        zs_buf[k] = total
-        for d in near(nz):
-            to = lax.rem(z + d, nz)
-            start(zs_buf.at[k, at(to * sub, sub)], zr_buf.at[k, z], zr_sem.at[k], dev(x, to, core))
-        zr_buf[k, z] = zs_buf[k, at(z * sub, sub), :]
-
-    def after_z(k):
-        wait(zr_buf.at[k, pl.ds(0, nz - 1)], zr_sem.at[k])
-        total = zr_buf[k, 0]
-        for j in range(1, nz):
-            total = total + zr_buf[k, j]
-        r = at(row_at(k, core, x, z), sub)
-        out_ref[r, :] = unit_rows(total)
-        for d in near(nz):
-            to = lax.rem(z + d, nz)
-            start(out_ref.at[r], out_ref.at[r], gz_sem.at[k], dev(x, to, core))
-
-    def forward(k, x_at):
-        ref = out_ref.at[at(row_at(k, core, x_at), blk)]
+    lax.fori_loop(0, last, products, 0)
+    send_buf[last, other] = sums(at(row_at(last, other), part))
+    to_twin(last).start()
+    scatter(last - 1)
+    send_buf[last, core] = sums(at(row_at(last, core), part))
+    scatter(last)
+
+    def total_of(ref, n):
+        rows = ref.shape[0] // n
+        total = ref[0:rows, :]
+        for j in range(1, n):
+            total = total + ref[j * rows:(j + 1) * rows, :]
+        return total
+
+    def after_first(k):
+        one, two = axes(k)
+        blk = part // one.n
+        wait(xr_buf.at[k, pl.ds(0, part - blk)], xr_sem.at[k])
+        zs_buf[k, 0:blk, :] = total_of(xr_buf.at[k], one.n)
+        for to, peer in two.peers():
+            start(zs_buf.at[k, at(to * sub, sub)], zr_buf.at[k, at(two.place * sub, sub)], zr_sem.at[k], peer)
+        zr_buf[k, at(two.place * sub, sub), :] = zs_buf[k, at(two.place * sub, sub), :]
+
+    def after_second(k):
+        one, two = axes(k)
+        blk = part // one.n
+        wait(zr_buf.at[k, pl.ds(0, blk - sub)], zr_sem.at[k])
+        r = at(row_at(k, core, one.place, two.place), sub)
+        out_ref[r, :] = unit_rows(total_of(zr_buf.at[k, pl.ds(0, blk)], two.n))
+        for _, peer in two.peers():
+            start(out_ref.at[r], out_ref.at[r], gz_sem.at[k], peer)
+
+    def after_gather_second(k):
+        one = axes(k)[0]
+        blk = part // one.n
+        wait(zr_buf.at[k, pl.ds(0, blk - sub)], gz_sem.at[k])
+        ref = out_ref.at[at(row_at(k, core, one.place), blk)]
+        for _, peer in one.peers():
+            start(ref, ref, gx_sem.at[k], peer)
+
+    def after_gather_first(k):
+        wait(xr_buf.at[k, pl.ds(0, part - part // axes(k)[0].n)], gx_sem.at[k])
+        ref = out_ref.at[at(row_at(k, core), part)]
         start(ref, ref, gc_sem.at[k], twin)
 
-    def after_gather_z(k):
-        wait(zr_buf.at[k, pl.ds(0, nz - 1)], gz_sem.at[k])
-        ref = out_ref.at[at(row_at(k, core, x), blk)]
-        for d in near(nx):
-            to = lax.rem(x + d, nx)
-            start(ref, ref, gx_sem.at[k], dev(to, z, core))
-        forward(k, x)
-
-    def after_gather_x(k):
-        wait(xr_buf.at[k, pl.ds(0, nx - 1)], gx_sem.at[k])
-        for d in range(1, nx):
-            forward(k, lax.rem(x + d, nx))
-
-    for k in range(CHUNKS):
-        after_x(k)
+    def leave(k):
+        r = at(k * size, size)
+        return pltpu.make_async_copy(out_ref.at[r], out_hbm.at[r], out_sem.at[k])
+
+    order = [k for k in range(CHUNKS) if k not in Z_FIRST] + list(Z_FIRST)
+    for k in order:
+        after_first(k)
 
     def numer_pass(i, acc):
         for g in range(step_r // 8):
@@ -286,22 +326,41 @@
 
     numer = jnp.sum(lax.fori_loop(0, 2 * steps, numer_pass, zero), axis=0, keepdims=True)
     numer = sum_cols(ITERS, numer)
-    for k in range(CHUNKS):
-        after_z(k)
+    order = list(Z_FIRST) + [k for k in range(CHUNKS) if k not in Z_FIRST]
+    for k in order:
+        after_second(k)
     sim_ref[...] = numer() / row_sum * (1.0 / INV_TEMP)
-    for k in range(CHUNKS):
-        after_gather_z(k)
-    for k in range(CHUNKS):
-        after_gather_x(k)
-    for k in range(CHUNKS):
-        wait(core_buf.at[k], gc_sem.at[k])
+    for k in order:
+        after_gather_second(k)
+    order = [k for k in range(CHUNKS - 1) if k not in Z_FIRST] + list(Z_FIRST) + [CHUNKS - 1]
+    done = None
+    for k in order + [None]:
+        if k is not None:
+            after_gather_first(k)
+        if done is not None:
+            wait(core_buf.at[done], gc_sem.at[done])
+            leave(done).start()
+        done = k
 
     for src, sem in sent:
         remote(src, src, sem.at[0], sem.at[1], twin).wait_send()
     for k in range(CHUNKS):
         to_twin(k).wait_send()
-        for d in range(1, nx):
-            remote(xr_buf.at[k, 0], xr_buf.at[k, 0], xr_sem.at[k, 0], xr_sem.at[k, 1], twin).wait_send()
+        ref = xr_buf.at[k, pl.ds(0, part - part // axes(k)[0].n)]
+        remote(ref, ref, xr_sem.at[k, 0], xr_sem.at[k, 1], twin).wait_send()
+        leave(k).wait()
+
+
+def hand_out(centres_ref, sim_ref, out_ref, expected_ref, sem):
+    rows = out_ref.shape[0] // 4
+    copies = [pltpu.make_async_copy(sim_ref, expected_ref, sem.at[4])]
+    for i in range(4):
+        r = pl.ds(i * rows, rows)
+        copies.append(pltpu.make_async_copy(centres_ref.at[r], out_ref.at[r], sem.at[i]))
+    for copy in copies:
+        copy.start()
+    for copy in copies:
+        copy.wait()
 
 
 def local(dims, embeddings, centres):
@@ -311,19 +370,18 @@
     half = clus // 2
     size = clus // CHUNKS
     part = size // 2
-    blk = part // nx
-    sub = blk // nz
     dma = pltpu.SemaphoreType.DMA
     new_centres, expected = pl.pallas_call(
         functools.partial(kernel, dims, mols * lax.axis_size("rows"), clus * lax.axis_size("cols")),
         out_shape=(jax.ShapeDtypeStruct((clus, emb), F32), jax.ShapeDtypeStruct((1, mols), F32)),
-        in_specs=[pl.BlockSpec(memory_space=pltpu.VMEM)] * 2,
-        out_specs=(pl.BlockSpec(memory_space=pltpu.VMEM),) * 2,
+        in_specs=[pl.BlockSpec(memory_space=pl.ANY)] * 2,
+        out_specs=(pl.BlockSpec(memory_space=pl.ANY), pl.BlockSpec(memory_space=pltpu.VMEM)),
         scratch_shapes=[
+            pltpu.VMEM((clus, emb), F32),
             pltpu.VMEM((clus, mols), F32),
             pltpu.VMEM((clus, mols), F32),
-            pltpu.VMEM((clus, 4 * emb), BF16),
-            pltpu.VMEM((mols, 4 * emb), BF16),
+            pltpu.VMEM((clus, 2 * emb), BF16),
+            pltpu.VMEM((mols, 2 * emb), BF16),
             pltpu.VMEM((mols, emb), F32),
             pltpu.VMEM((clus, 128), F32),
             pltpu.VMEM((clus, 128), F32),
@@ -333,9 +391,11 @@
             pltpu.VMEM((ITERS + 1, ny, 1, mols), F32),
             pltpu.VMEM((CHUNKS, part, emb), F32),
             pltpu.VMEM((CHUNKS, 2, part, emb), F32),
-            pltpu.VMEM((CHUNKS, nx, blk, emb), F32),
-            pltpu.VMEM((CHUNKS, blk, emb), F32),
-            pltpu.VMEM((CHUNKS, nz, sub, emb), F32),
+            pltpu.VMEM((CHUNKS, part, emb), F32),
+            pltpu.VMEM((CHUNKS, part // min(nx, nz), emb), F32),
+            pltpu.VMEM((CHUNKS, part // min(nx, nz), emb), F32),
+            dma((mols // min(256, mols), 2)),
+            dma((CHUNKS,)),
             dma((ITERS, 2)),
             dma((ITERS, 2)),
             dma((ITERS, 2)),
@@ -348,10 +408,17 @@
             dma((CHUNKS, 2)),
         ],
         compiler_params=pltpu.CompilerParams(
-            collective_id=0, has_side_effects=True, vmem_limit_bytes=60 * 1024 * 1024),
+            collective_id=0, has_side_effects=True, vmem_limit_bytes=62 * 1024 * 1024),
         cost_estimate=pl.CostEstimate(flops=2 * 8 * mols * clus * emb, bytes_accessed=4 * 1024 * 1024,
                                       transcendentals=mols * clus),
     )(embeddings, centres)
+    new_centres, expected = pl.pallas_call(
+        hand_out,
+        out_shape=(jax.ShapeDtypeStruct((clus, emb), F32), jax.ShapeDtypeStruct((1, mols), F32)),
+        in_specs=[pl.BlockSpec(memory_space=pltpu.VMEM)] * 2,
+        out_specs=(pl.BlockSpec(memory_space=pl.ANY),) * 2,
+        scratch_shapes=[dma((5,))],
+    )(new_centres, expected)
     return new_centres, expected.reshape(mols)
 
 

time: 90.3 us -> 85.5 us (0.947)
  local copies, waits for them, and re-layouts: 2.87 us -> 0 us
  Pallas kernels: 86.7 us -> 84.8 us
    pallas_call x1, Pallas kernels: 86.7 us -> 82.5 us  [local(): pl.pallas_call(functools.partial(kernel, dims, mols * lax.axis_size('rows...]
    unnamed x4 -> x0, local copies, waits for them, and re-layouts: 2.87 us -> none
    pallas_call x0 -> x1, Pallas kernels: none -> 2.24 us  [local(): pl.pallas_call(hand_out, out_shape=(jax.ShapeDtypeStruct((clus, emb), F32...]
where the time goes in v3:
time: 85.5 us; the launch traced here: 85.4 us
  Pallas kernels  84.8 us (99%)
    pallas_call x1, Pallas kernels, local(): pl.pallas_call(functools.partial(kernel, dims, mols * lax.axis_size('rows...  82.5 us
    pallas_call x1, Pallas kernels, local(): pl.pallas_call(hand_out, out_shape=(jax.ShapeDtypeStruct((clus, emb), F32...  2.24 us

profile of v3, /device:TPU:1, one launch (start us, length us, event | category | flops | bytes accessed | tf_op | source)
XLA Modules:
  0.0 85.4 jit_solution(8571716012405850310)
XLA Ops:
  0.6 82.5 %shard_map.41 = (f32[2048,128]{1,0:T(8,128)}, f32[1,2048]{1,0:T(1,128)}) custom-call(f32[2048,128]{1,0:T(8,128)} %x_hbm.1, f32[2048,128]{1,0:T(8,128)} %c_hbm.1), custom_call_target="tpu_custom_call" | custom-call | flops 8589934592 | bytes 4194304 | tf_op jit(solution)/shard_map/pallas_call | solution.py:374
  83.2 2.2 %shard_map.42 = (f32[2048,128]{1,0:T(8,128)}, f32[1,2048]{1,0:T(1,128)}) custom-call(f32[2048,128]{1,0:T(8,128)} %get-tuple-element.6.centres_ref, f32[1,2048]{1,0:T(1,128)} %get-tuple-element.7.sim_ref), custom_call_target="tpu_custom_call" | custom-call | tf_op jit(solution)/shard_map/pallas_call | solution.py:415

commit v4 on v3

--- a/solution.py
+++ b/solution.py
@@ -15,7 +15,8 @@
 MESH = pl.DeviceIdType.MESH
 CHIPS_X, CHIPS_Z, CHIPS_Y = 4, 8, 4
 CHUNKS = 4
-Z_FIRST = (0,)
+Z_FIRST = ()
+ONE_SHOT = (2, 3)
 
 
 def split(value):
@@ -80,16 +81,19 @@
         return pltpu.make_async_remote_copy(
             src_ref=src, dst_ref=dst, send_sem=send, recv_sem=recv, device_id=to, device_id_type=MESH)
 
-    sent = []
-
-    def start(src, dst, sem, to, keep=True):
-        copy = remote(src, dst, sem.at[0], sem.at[1], to)
-        copy.start()
-        if keep:
-            sent.append((src, sem))
+    def start(src, dst, sem, to):
+        remote(src, dst, sem.at[0], sem.at[1], to).start()
+
+    received = []
 
     def wait(ref, sem):
         remote(ref, ref, sem.at[0], sem.at[1], twin).wait_recv()
+        received.append((ref, sem))
+
+    def drain():
+        for ref, sem in received:
+            remote(ref, ref, sem.at[0], sem.at[1], twin).wait_send()
+        received.clear()
 
     def at(start_row, size):
         return pl.ds(pl.multiple_of(start_row, size), size)
@@ -126,7 +130,7 @@
 
     lax.fori_loop(0, clus // row_b, score, 0)
 
-    step_r = min(128, half)
+    step_r = min(256, half)
     steps = half // step_r
     zero = jnp.zeros((8, mols), F32)
 
@@ -247,8 +251,7 @@
         to_twin(k).wait_recv()
         send_buf[k, core] = send_buf[k, core] + core_buf[k]
         for to, peer in one.peers():
-            start(send_buf.at[k, core, at(to * blk, blk)], xr_buf.at[k, at(one.place * blk, blk)], xr_sem.at[k], peer,
-                  False)
+            start(send_buf.at[k, core, at(to * blk, blk)], xr_buf.at[k, at(one.place * blk, blk)], xr_sem.at[k], peer)
         xr_buf[k, at(one.place * blk, blk), :] = send_buf[k, core, at(one.place * blk, blk), :]
 
     last = CHUNKS - 1
@@ -294,6 +297,10 @@
         wait(zr_buf.at[k, pl.ds(0, blk - sub)], zr_sem.at[k])
         r = at(row_at(k, core, one.place, two.place), sub)
         out_ref[r, :] = unit_rows(total_of(zr_buf.at[k, pl.ds(0, blk)], two.n))
+        if k in ONE_SHOT:
+            for p in away:
+                start(out_ref.at[r], out_ref.at[r], gx_sem.at[k], dev(*chip_at(p), core))
+            return
         for _, peer in two.peers():
             start(out_ref.at[r], out_ref.at[r], gz_sem.at[k], peer)
 
@@ -306,17 +313,14 @@
             start(ref, ref, gx_sem.at[k], peer)
 
     def after_gather_first(k):
-        wait(xr_buf.at[k, pl.ds(0, part - part // axes(k)[0].n)], gx_sem.at[k])
+        own = sub if k in ONE_SHOT else part // axes(k)[0].n
+        wait(xr_buf.at[k, pl.ds(0, part - own)], gx_sem.at[k])
         ref = out_ref.at[at(row_at(k, core), part)]
         start(ref, ref, gc_sem.at[k], twin)
 
     def leave(k):
         r = at(k * size, size)
         return pltpu.make_async_copy(out_ref.at[r], out_hbm.at[r], out_sem.at[k])
-
-    order = [k for k in range(CHUNKS) if k not in Z_FIRST] + list(Z_FIRST)
-    for k in order:
-        after_first(k)
 
     def numer_pass(i, acc):
         for g in range(step_r // 8):
@@ -324,30 +328,44 @@
             acc = acc + scaled(r) * t_ref[r, :]
         return acc
 
-    numer = jnp.sum(lax.fori_loop(0, 2 * steps, numer_pass, zero), axis=0, keepdims=True)
-    numer = sum_cols(ITERS, numer)
-    order = list(Z_FIRST) + [k for k in range(CHUNKS) if k not in Z_FIRST]
-    for k in order:
-        after_second(k)
+    pieces = 4
+    numer = zero
+
+    def numer_piece(i):
+        return lax.fori_loop(2 * steps * i // pieces, 2 * steps * (i + 1) // pieces, numer_pass, numer)
+
+    def end(k):
+        wait(core_buf.at[k], gc_sem.at[k])
+        leave(k).start()
+
+    after_first(0)
+    numer = numer_piece(0)
+    after_first(1)
+    numer = numer_piece(1)
+    after_first(2)
+    numer = numer_piece(2)
+    after_first(3)
+    after_second(0)
+    numer = numer_piece(3)
+    numer = sum_cols(ITERS, jnp.sum(numer, axis=0, keepdims=True))
+    after_second(1)
+    after_second(2)
+    after_second(3)
+    after_gather_second(0)
+    after_gather_second(1)
     sim_ref[...] = numer() / row_sum * (1.0 / INV_TEMP)
-    for k in order:
-        after_gather_second(k)
-    order = [k for k in range(CHUNKS - 1) if k not in Z_FIRST] + list(Z_FIRST) + [CHUNKS - 1]
-    done = None
-    for k in order + [None]:
-        if k is not None:
-            after_gather_first(k)
-        if done is not None:
-            wait(core_buf.at[done], gc_sem.at[done])
-            leave(done).start()
-        done = k
-
-    for src, sem in sent:
-        remote(src, src, sem.at[0], sem.at[1], twin).wait_send()
+    after_gather_first(0)
+    after_gather_first(1)
+    end(0)
+    after_gather_first(2)
+    end(1)
+    after_gather_first(3)
+    end(2)
+    end(3)
+
+    drain()
     for k in range(CHUNKS):
         to_twin(k).wait_send()
-        ref = xr_buf.at[k, pl.ds(0, part - part // axes(k)[0].n)]
-        remote(ref, ref, xr_sem.at[k, 0], xr_sem.at[k, 1], twin).wait_send()
         leave(k).wait()
 
 

time: 85.5 us -> 84 us (0.982)
  Pallas kernels: 84.8 us -> 83.2 us
    pallas_call x1, Pallas kernels: 82.5 us -> 81 us  [local(): pl.pallas_call(functools.partial(kernel, dims, mols * lax.axis_size('rows...]
where the time goes in v4:
time: 84 us; the launch traced here: 83.8 us
  Pallas kernels  83.2 us (99%)
    pallas_call x1, Pallas kernels, local(): pl.pallas_call(functools.partial(kernel, dims, mols * lax.axis_size('rows...  81 us
    pallas_call x1, Pallas kernels, local(): pl.pallas_call(hand_out, out_shape=(jax.ShapeDtypeStruct((clus, emb), F32...  2.24 us

profile of v4, /device:TPU:1, one launch (start us, length us, event | category | flops | bytes accessed | tf_op | source)
XLA Modules:
  0.0 83.8 jit_solution(13642212011695914640)
XLA Ops:
  0.6 81.0 %shard_map.41 = (f32[2048,128]{1,0:T(8,128)}, f32[1,2048]{1,0:T(1,128)}) custom-call(f32[2048,128]{1,0:T(8,128)} %x_hbm.1, f32[2048,128]{1,0:T(8,128)} %c_hbm.1), custom_call_target="tpu_custom_call" | custom-call | flops 8589934592 | bytes 4194304 | tf_op jit(solution)/shard_map/pallas_call | solution.py:392
  81.6 2.2 %shard_map.42 = (f32[2048,128]{1,0:T(8,128)}, f32[1,2048]{1,0:T(1,128)}) custom-call(f32[2048,128]{1,0:T(8,128)} %get-tuple-element.6.centres_ref, f32[1,2048]{1,0:T(1,128)} %get-tuple-element.7.sim_ref), custom_call_target="tpu_custom_call" | custom-call | tf_op jit(solution)/shard_map/pallas_call | solution.py:433

commit v5 on v4

--- a/solution.py
+++ b/solution.py
@@ -130,7 +130,7 @@
 
     lax.fori_loop(0, clus // row_b, score, 0)
 
-    step_r = min(256, half)
+    step_r = min(512, half)
     steps = half // step_r
     zero = jnp.zeros((8, mols), F32)
 
@@ -256,23 +256,23 @@
 
     last = CHUNKS - 1
 
-    def products(k, _):
-        both = sums(at(k * size, size))
-        send_buf[k, 0] = both[0:part]
-        send_buf[k, 1] = both[part:size]
-        to_twin(k).start()
-        for done in range(last - 1):
-            @pl.when(k == done + 1)
+    def products(i, _):
+        k, own = lax.div(i, 2), lax.rem(i, 2)
+        which = lax.rem(core + 1 + own, 2)
+        send_buf[k, which] = sums(at(row_at(k, which), part))
+
+        @pl.when(own == 0)
+        def _():
+            to_twin(k).start()
+
+        for done in range(last):
+            @pl.when(i == 2 * done + 2)
             def _():
                 scatter(done)
 
         return 0
 
-    lax.fori_loop(0, last, products, 0)
-    send_buf[last, other] = sums(at(row_at(last, other), part))
-    to_twin(last).start()
-    scatter(last - 1)
-    send_buf[last, core] = sums(at(row_at(last, core), part))
+    lax.fori_loop(0, 2 * CHUNKS, products, 0)
     scatter(last)
 
     def total_of(ref, n):
@@ -317,10 +317,11 @@
         wait(xr_buf.at[k, pl.ds(0, part - own)], gx_sem.at[k])
         ref = out_ref.at[at(row_at(k, core), part)]
         start(ref, ref, gc_sem.at[k], twin)
-
-    def leave(k):
-        r = at(k * size, size)
-        return pltpu.make_async_copy(out_ref.at[r], out_hbm.at[r], out_sem.at[k])
+        leave(k, core).start()
+
+    def leave(k, core_at):
+        r = at(row_at(k, core_at), part)
+        return pltpu.make_async_copy(out_ref.at[r], out_hbm.at[r], out_sem.at[k, core_at])
 
     def numer_pass(i, acc):
         for g in range(step_r // 8):
@@ -336,15 +337,15 @@
 
     def end(k):
         wait(core_buf.at[k], gc_sem.at[k])
-        leave(k).start()
+        leave(k, other).start()
 
     after_first(0)
+    after_first(1)
     numer = numer_piece(0)
-    after_first(1)
+    after_first(2)
     numer = numer_piece(1)
-    after_first(2)
+    after_first(3)
     numer = numer_piece(2)
-    after_first(3)
     after_second(0)
     numer = numer_piece(3)
     numer = sum_cols(ITERS, jnp.sum(numer, axis=0, keepdims=True))
@@ -366,7 +367,8 @@
     drain()
     for k in range(CHUNKS):
         to_twin(k).wait_send()
-        leave(k).wait()
+        leave(k, 0).wait()
+        leave(k, 1).wait()
 
 
 def hand_out(centres_ref, sim_ref, out_ref, expected_ref, sem):
@@ -413,7 +415,7 @@
             pltpu.VMEM((CHUNKS, part // min(nx, nz), emb), F32),
             pltpu.VMEM((CHUNKS, part // min(nx, nz), emb), F32),
             dma((mols // min(256, mols), 2)),
-            dma((CHUNKS,)),
+            dma((CHUNKS, 2)),
             dma((ITERS, 2)),
             dma((ITERS, 2)),
             dma((ITERS, 2)),

time: 84 us -> 83.3 us (level)
  no operation moved by 1% of the time
where the time goes in v5:
time: 83.3 us; the launch traced here: 83.2 us
  Pallas kernels  82.6 us (99%)
    pallas_call x1, Pallas kernels, local(): pl.pallas_call(functools.partial(kernel, dims, mols * lax.axis_size('rows...  80.3 us
    pallas_call x1, Pallas kernels, local(): pl.pallas_call(hand_out, out_shape=(jax.ShapeDtypeStruct((clus, emb), F32...  2.24 us

profile of v5, /device:TPU:1, one launch (start us, length us, event | category | flops | bytes accessed | tf_op | source)
XLA Modules:
  0.0 83.2 jit_solution(17776578716156183638)
XLA Ops:
  0.6 80.3 %shard_map.41 = (f32[2048,128]{1,0:T(8,128)}, f32[1,2048]{1,0:T(1,128)}) custom-call(f32[2048,128]{1,0:T(8,128)} %x_hbm.1, f32[2048,128]{1,0:T(8,128)} %c_hbm.1), custom_call_target="tpu_custom_call" | custom-call | flops 8589934592 | bytes 4194304 | tf_op jit(solution)/shard_map/pallas_call | solution.py:394
  81.0 2.2 %shard_map.42 = (f32[2048,128]{1,0:T(8,128)}, f32[1,2048]{1,0:T(1,128)}) custom-call(f32[2048,128]{1,0:T(8,128)} %get-tuple-element.6.centres_ref, f32[1,2048]{1,0:T(1,128)} %get-tuple-element.7.sim_ref), custom_call_target="tpu_custom_call" | custom-call | tf_op jit(solution)/shard_map/pallas_call | solution.py:435
